TPU v7x, 32 devices: a whole 2x2x4 slice. The times are simulated.
32 devices in a mesh: vocab: 16 (over z, y, x), rows: 2 (over core).
Axes of the slice: x: 2, y: 2, z: 4, core: 2. Of those that a mesh axis runs over, the one named last changes fastest.
Arguments:
- hidden: bfloat16 [1024, 4096], P('rows', 'vocab'), may hold values from -48 to 48
- head_weight: bfloat16 [4096, 16384], P('rows', 'vocab'), may hold values from -1 to 1
- in_proj: bfloat16 [4096, 64], replicated, may hold values from -0.09375 to 0.09375
- out_proj: bfloat16 [16384, 64], P('vocab'), may hold values from -6 to 6
- targets: int32 [1024], P('rows'), may hold values from 0 to 16383
- lengths: int32 [8], replicated, may hold values from 1 to 128, as said below
- grad_store: bfloat16 [8192, 4096], P(('vocab', 'rows')), may hold values from -0.09375 to 0.09375
Outputs:
- scores: float32 [8, 8192], P(None, ('vocab', 'rows'))
Inputs may be any that keep to these rules, and one draw needn't show every extreme that they name: `lengths`: at least one sequence has exactly 128 valid rows.
All inputs are finite; a program needn't handle non-finite values.
Results may differ from a plain program's by a relative error of at most 0.0029.
Values may be sent and summed in bfloat16 or wider, within the bound.
A program may use at most 64 MiB of HBM per device.

v0:
```python
import jax
import jax.numpy as jnp
from jax import lax
from jax.sharding import PartitionSpec as P

TILE = 128


damping_ratio = 0.1
tiny_value = 1e-06


def joined(value, axis, join):
    pieces = jax.tree.map(lambda part: lax.all_gather(part, axis), value)
    head = jax.tree.map(lambda part: part[0], pieces)
    tail = jax.tree.map(lambda part: part[1:], pieces)
    running, _ = lax.scan(lambda running, slab: (join(running, slab), None), head, tail)
    return running


def whiten(seq_grads, cov_out, cov_in):
    proj_width = cov_out.shape[0]
    seq_count = seq_grads.shape[0]
    identity = jnp.eye(proj_width, dtype=jnp.float32)
    damp_out = damping_ratio * jnp.trace(cov_out) / proj_width + tiny_value
    damp_in = damping_ratio * jnp.trace(cov_in) / proj_width + tiny_value
    lower_out = jnp.linalg.cholesky(cov_out + damp_out * identity)
    lower_in = jnp.linalg.cholesky(cov_in + damp_in * identity)
    stacked = jnp.transpose(seq_grads, (1, 0, 2)).reshape(proj_width, seq_count * proj_width)
    left_half = lax.linalg.triangular_solve(lower_out, stacked, left_side=True, lower=True)
    left_full = lax.linalg.triangular_solve(
        lower_out, left_half, left_side=True, lower=True, transpose_a=True
    )
    rows_form = jnp.transpose(
        left_full.reshape(proj_width, seq_count, proj_width), (1, 0, 2)
    ).reshape(seq_count * proj_width, proj_width)
    right_half = lax.linalg.triangular_solve(
        lower_in, rows_form, left_side=False, lower=True, transpose_a=True
    )
    right_full = lax.linalg.triangular_solve(lower_in, right_half, left_side=False, lower=True)
    return right_full.reshape(seq_count, proj_width * proj_width)


def combine_rows(earlier, later):
    max_one, sum_one, weight_one = earlier
    max_two, sum_two, weight_two = later
    joint_max = jnp.maximum(max_one, max_two)
    scale_one = jnp.exp(max_one - joint_max)
    scale_two = jnp.exp(max_two - joint_max)
    joint_sum = sum_one * scale_one + sum_two * scale_two
    joint_weight = weight_one * scale_one[:, None] + weight_two * scale_two[:, None]
    return (joint_max, joint_sum, joint_weight)


def per_device(hidden, head_weight, in_proj, out_proj, targets, lengths, grad_store):
    token_count = hidden.shape[0]
    vocab_cols = head_weight.shape[1]
    proj_width = in_proj.shape[1]
    tile_count = token_count // TILE
    features = lax.all_gather(hidden, "vocab", axis=1, tiled=True)
    out_table = out_proj.astype(jnp.float32)
    first_column = lax.axis_index("vocab") * vocab_cols
    column_ids = lax.broadcasted_iota(jnp.int32, (token_count, vocab_cols), 1) + first_column
    onehot = (column_ids == targets[:, None]).astype(jnp.float32)
    picked_local = jnp.dot(onehot, out_table, precision=lax.Precision.HIGHEST)
    picked = lax.psum(picked_local, "vocab")
    logits = jnp.dot(
        features,
        lax.all_gather(head_weight, "rows", axis=0, tiled=True),
        preferred_element_type=jnp.float32,
    )
    local_max = jnp.max(logits, axis=1)
    exponent = jnp.exp(logits - local_max[:, None])
    weighted = jnp.dot(exponent, out_table, precision=lax.Precision.HIGHEST)
    merged = joined((local_max, jnp.sum(exponent, axis=1), weighted), "vocab", combine_rows)
    out_grad = merged[2] / merged[1][:, None] - picked
    input_proj = jnp.dot(features, in_proj, preferred_element_type=jnp.float32)
    own_lengths = lax.dynamic_slice_in_dim(lengths, lax.axis_index("rows") * tile_count, tile_count)
    position = lax.broadcasted_iota(jnp.int32, (tile_count, TILE), 1)
    is_valid = (position < own_lengths[:, None]).astype(jnp.float32)[:, :, None]
    out_tiles = out_grad.reshape(tile_count, TILE, proj_width) * is_valid
    in_tiles = input_proj.reshape(tile_count, TILE, proj_width) * is_valid
    flat_out = out_tiles.reshape(token_count, proj_width)
    flat_in = in_tiles.reshape(token_count, proj_width)
    local_out = jnp.dot(flat_out.T, flat_out, precision=lax.Precision.HIGHEST)
    local_in = jnp.dot(flat_in.T, flat_in, precision=lax.Precision.HIGHEST)
    cov_out, cov_in = lax.psum((local_out, local_in), "rows")
    row_total = jnp.sum(lengths).astype(jnp.float32)
    seq_grads = jnp.einsum("stk,stj->skj", out_tiles, in_tiles, precision=lax.Precision.HIGHEST)
    seq_grads = seq_grads / jnp.sqrt(own_lengths.astype(jnp.float32))[:, None, None]
    whitened = whiten(seq_grads, cov_out / row_total, cov_in / row_total).astype(jnp.bfloat16)
    return jnp.dot(
        lax.all_gather(whitened, "rows", axis=0, tiled=True),
        grad_store.T,
        preferred_element_type=jnp.float32,
    )


def solution(mesh):
    return jax.shard_map(
        per_device,
        mesh=mesh,
        in_specs=(
            P("rows", "vocab"),
            P("rows", "vocab"),
            P(),
            P("vocab", None),
            P("rows"),
            P(),
            P(("vocab", "rows"), None),
        ),
        out_specs=P(None, ("vocab", "rows")),
        check_vma=False,
    )
```

profile of v0, /device:TPU:1, one launch (start us, length us, event | category | flops | bytes accessed | tf_op | source)
XLA Modules:
  0.0 345.8 jit_solution(6807098756265005803)
XLA Ops:
  6.5 0.7 all-gather.10.cloned.1.call-update
  7.3 0.7 all-gather.12.cloned.1.call-update
  8.1 90.6 %all-gather.10.cloned.1.call-done = bf16[512,4096]{1,0:T(8,128)(2,1)} async-done(((bf16[512,256]{1,0:T(8,128)(2,1)}), bf16[512,4096]{1,0:T(8,128)(2,1)}) %all-gather.10.cloned.1.call-update) | async-done | bytes 4194320 | tf_op jit(solution)/shard_map/all_gather | solution.py:60
  98.6 20.7 %all-gather.12.cloned.1.call-done = bf16[4096,1024]{1,0:T(8,128)(2,1)} async-done(((bf16[2048,1024]{1,0:T(8,128)(2,1)}), bf16[4096,1024]{1,0:T(8,128)(2,1)}) %all-gather.12.cloned.1.call-update) | async-done | bytes 8388624 | tf_op jit(solution)/shard_map/all_gather | solution.py:69
  119.3 8.3 %fusion.40 = (f32[512]{0:T(512)S(1)}, f32[512,1024]{1,0:T(8,128)S(1)}) fusion(bf16[512,4096]{1,0:T(8,128)(2,1)} %all-gather.10.cloned.1.call-done, bf16[4096,1024]{1,0:T(8,128)(2,1)} %all-gather.12.cloned.1.call-done), kind=kOutput, calls=%fused_computation.69 | convolution fusion | flops 4295491072 | bytes 14682112 | tf_op jit(solution)/shard_map/dot_general | solution.py:67
  127.7 1.3 copy-done.1
  129.0 2.1 fusion.3
  131.2 1.2 fusion.1
  132.5 0.6 reduce_sum.35
  133.1 0.1 convert_sqrt_fusion
  133.2 0.1 fusion.38
  133.8 3.7 %fusion.41 = f32[512,64]{0,1:T(8,128)S(1)} fusion(bf16[512,4096]{1,0:T(8,128)(2,1)} %all-gather.10.cloned.1.call-done, bf16[4096,64]{0,1:T(8,128)(2,1)S(1)} %copy-done.3), kind=kOutput, calls=%fused_computation.70 | convolution fusion | flops 268435456 | bytes 4849664 | tf_op jit(solution)/shard_map/dot_general | solution.py:77
  137.6 0.3 fusion.11
  137.8 0.5 fusion.4
  138.3 34.0 %all-gather.4 = f32[16,1,512]{2,1,0:T(1,128)S(1)} all-gather(f32[1,1,512]{2,1,0:T(1,128)S(1)} %bitcast.94), channel_id=3, replica_groups=mesh['vocab'=16,'rows'=2] {'vocab'}, dimensions={0}, use_global_device_ids=true | all-gather | bytes 34816 | tf_op jit(solution)/shard_map/all_gather | solution.py:14
  172.3 29.0 %all-gather.3 = f32[16,1,512]{2,1,0:T(1,128)S(1)} all-gather(f32[1,1,512]{2,1,0:T(1,128)S(1)} %bitcast.93), channel_id=2, replica_groups=mesh['vocab'=16,'rows'=2] {'vocab'}, dimensions={0}, use_global_device_ids=true | all-gather | bytes 34816 | tf_op jit(solution)/shard_map/all_gather | solution.py:14
  201.4 3.0 slice.59
  204.4 3.7 %copy.42 = f32[7680,64]{1,0:T(8,128)} copy(f32[7680,64]{0,1:T(8,128)} %slice.59) | data formatting | bytes 3932160 | tf_op jit(solution)/shard_map/while | solution.py:17
  208.1 0.1 copy.28
  208.3 19.0 %while.14 = (s32[]{:T(128)}, f32[512]{0:T(512)S(1)}, f32[512]{0:T(512)S(1)}, f32[512,64]{1,0:T(8,128)S(1)}, f32[15,512]{1,0:T(8,128)S(1)}, /*index=5*/f32[15,512]{1,0:T(8,128)S(1)}, f32[15,512,64]{2,1,0:T(8,128)}, s32[]{:T(128)}) while((s32[]{:T(128)}, f32[512]{0:T(512)S(1)}, f32[512]{0:T(512)S(1)}, f32[512,64]{1,0:T(8,128)S(1)}, ...), condition=%wide.region_3.4_spmd, body=%wide.region_2.0_spmd.sunk | while | flops 101378 | bytes 421981 | solution.py:17
  208.3 1.2 fusion.59
  209.6 1.2 fusion.59
  210.8 1.2 fusion.59
  212.1 1.2 fusion.59
  213.4 1.2 fusion.59
  214.6 1.2 fusion.59
  215.9 1.2 fusion.59
  217.2 1.2 fusion.59
  218.4 1.2 fusion.59
  219.7 1.2 fusion.59
  221.0 1.2 fusion.59
  222.2 1.2 fusion.59
  223.5 1.2 fusion.59
  224.8 1.2 fusion.59
  226.0 1.2 fusion.59
  227.3 0.1 copy.30
  227.4 71.6 %all-reduce.3.cloned.1.call-done = f32[512,64]{0,1:T(8,128)} async-done(((f32[512,64]{0,1:T(8,128)}), f32[512,64]{0,1:T(8,128)}) %all-reduce.3.cloned.1.call-update) | async-done | bytes 131088 | tf_op jit(solution)/shard_map/psum | solution.py:66
  299.0 1.2 fusion.13
  300.2 6.0 %all-reduce = (f32[64,64]{1,0:T(8,128)S(1)}, f32[64,64]{1,0:T(8,128)S(1)}) all-reduce(f32[64,64]{1,0:T(8,128)S(1)} %fusion.13, f32[64,64]{1,0:T(8,128)S(1)} %fusion.11), channel_id=1, replica_groups=mesh['vocab'=16,'rows'=2] {'rows'}, use_global_device_ids=true, to_apply=%region_5.6 | all-reduce | flops 8192 | bytes 65536 | tf_op jit(solution)/shard_map/psum | solution.py:87
  306.2 0.7 fusion.33
  307.6 0.1 copy.38
  307.7 0.1 copy.39
  307.8 5.9 %cholesky.55 = f32[64,64]{1,0:T(8,128)S(1)} custom-call(f32[64,64]{1,0:T(8,128)S(1)} %copy.39), custom_call_target="Cholesky" | custom-call | tf_op jit(solution)/shard_map/jit(cholesky)/cholesky | solution.py:28
  313.7 0.7 compare_reduce_fusion
  314.4 0.7 fusion.19
  315.1 4.9 %custom-call.13 = f32[1,64,64]{1,2,0:T(8,128)S(1)} custom-call(f32[1,64,64]{2,1,0:T(8,128)S(1)} %fusion.19), custom_call_target="InvertDiagBlocksLowerTriangular" | custom-call | tf_op jit(solution)/shard_map/triangular_solve | solution.py:37
  320.7 0.1 copy.31
  320.8 0.1 copy.32
  320.9 5.9 %cholesky.44 = f32[64,64]{1,0:T(8,128)S(1)} custom-call(f32[64,64]{1,0:T(8,128)S(1)} %copy.32), custom_call_target="Cholesky" | custom-call | tf_op jit(solution)/shard_map/jit(cholesky)/cholesky | solution.py:27
  326.8 0.6 compare_reduce_fusion.1
  327.4 0.7 fusion.18
  328.1 4.9 %custom-call.12 = f32[1,64,64]{1,2,0:T(8,128)S(1)} custom-call(f32[1,64,64]{2,1,0:T(8,128)S(1)} %fusion.18), custom_call_target="InvertDiagBlocksLowerTriangular" | custom-call | tf_op jit(solution)/shard_map/triangular_solve | solution.py:31
  333.0 1.3 fusion.5
  334.2 0.1 copy.35
  334.3 0.1 reshape.78
  334.5 0.1 copy.43
  334.6 0.3 fusion.24
  334.8 0.5 fusion.26
  335.3 0.3 fusion.21
  335.6 0.2 convolution_convert_fusion
  335.8 0.1 copy.40
  336.0 0.1 reshape.97
  336.1 1.9 all-gather.5
  338.0 1.3 fusion.42
  (66 shorter events, 0.9 us)
Async XLA Ops:
  6.5 331.4 %copy-start = (bf16[256,4096]{1,0:T(8,128)(2,1)S(1)}, bf16[256,4096]{1,0:T(8,128)(2,1)}, u32[]{:S(2)}) copy-start(bf16[256,4096]{1,0:T(8,128)(2,1)} %param.16) | copy-start | bytes 6291460
  6.5 92.1 %all-gather.10.cloned.1.call-start = ((), (), s32[]{:S(2)}) async-start(), calls=%async_computation | async-start | bytes 4456448 | tf_op jit(solution)/shard_map/all_gather | solution.py:60
  7.3 112.1 %all-gather.12.cloned.1.call-start = ((), (), s32[]{:S(2)}) async-start(), calls=%async_computation.1 | async-start | bytes 12582912 | tf_op jit(solution)/shard_map/all_gather | solution.py:69
  8.0 121.0 %copy-start.4 = (bf16[1024,64]{0,1:T(8,128)(2,1)S(1)}, bf16[1024,64]{0,1:T(8,128)(2,1)}, u32[]{:S(2)}) copy-start(bf16[1024,64]{0,1:T(8,128)(2,1)} %param.13) | copy-start | bytes 393220
  8.0 193.4 %all-gather.14.cloned.1.call-start = ((), (), s32[]{:S(2)}) async-start(), calls=%async_computation.3 | async-start | bytes 2228224 | tf_op jit(solution)/shard_map/all_gather | solution.py:14
  127.7 1.3 copy-start.1
  127.7 3.5 %copy-start.6 = (s32[512]{0:T(512)S(1)}, s32[512]{0:T(512)}, u32[]{:S(2)}) copy-start(s32[512]{0:T(512)} %param.14) | copy-start | bytes 6148
  127.7 4.8 %copy-start.5 = (s32[8]{0:T(128)S(1)}, s32[8]{0:T(128)}, u32[]{:S(2)}) copy-start(s32[8]{0:T(128)} %param.15) | copy-start | bytes 100
  127.7 6.1 %copy-start.3 = (bf16[4096,64]{0,1:T(8,128)(2,1)S(1)}, bf16[4096,64]{0,1:T(8,128)(2,1)}, u32[]{:S(2)}) copy-start(bf16[4096,64]{0,1:T(8,128)(2,1)} %param.12) | copy-start | bytes 1572868
  131.1 167.8 %all-reduce.3.cloned.1.call-start = ((), (), s32[]{:S(2)}) async-start(), calls=%async_computation.2 | async-start | bytes 262144 | tf_op jit(solution)/shard_map/psum | solution.py:66
  133.8 4.0 %copy-start.2 = (f32[512,1024]{1,0:T(8,128)S(1)}, f32[512,1024]{1,0:T(8,128)}, u32[]{:S(2)}) copy-start(f32[512,1024]{1,0:T(8,128)} %copy-done.1) | copy-start | bytes 6291460
  204.4 3.7 %slice-start = ((f32[8192,64]{0,1:T(8,128)}), f32[512,64]{0,1:T(8,128)S(1)}, s32[]{:S(2)}) async-start(f32[8192,64]{0,1:T(8,128)} %all-gather.14.cloned.1.call-done), calls=%async_computation.4 | async-start | bytes 262144 | tf_op jit(solution)/shard_map/slice | solution.py:15
Sparse Core Ops, SparseCore 0:
  10.1 88.5 all-gather.9
  100.2 19.1 all-gather.11
  131.2 60.6 all-gather.13
  197.2 101.6 all-reduce.2
where the time goes:
time: 347 us; the launch traced here: 346 us
  waiting for transfers between devices  184 us (53%)
  blocking collectives  70.9 us (20%)
  other arithmetic  44.7 us (13%)
  matrix products  20.7 us (6%)
  between operations  15.4 us (4%)
  local copies, waits for them, and re-layouts  9.29 us (3%)
    all_gather x1, waiting for transfers between devices, per_device(): features = lax.all_gather(hidden, 'vocab', axis=1, tiled=True)  90.6 us
    psum x1, waiting for transfers between devices, per_device(): picked = lax.psum(picked_local, 'vocab')  71.6 us
    all_gather x2, blocking collectives, joined(): pieces = jax.tree.map(lambda part: lax.all_gather(part, axis), value)  63 us
    all_gather x1, waiting for transfers between devices, per_device(): lax.all_gather(head_weight, 'rows', axis=0, tiled=True)  20.7 us
    add x15, other arithmetic, combine_rows(): weight_one * scale_one[:, None] + weight_two * scale_two[:, None]  18.1 us
    dot_general x1, matrix products, per_device(): jnp.dot(features, lax.all_gather(head_weight, 'rows', axis=0, tiled=True)...  8.3 us
  transfers between devices with their start and end apart: 4, of which 3 were waited for; matrix products, arithmetic and copies ran while one was open for 9% of the time, Pallas kernels for 0%

commit v1 on v0

--- a/solution.py
+++ b/solution.py
@@ -1,6 +1,10 @@
+import functools
+
 import jax
 import jax.numpy as jnp
 from jax import lax
+from jax.experimental import pallas as pl
+from jax.experimental.pallas import tpu as pltpu
 from jax.sharding import PartitionSpec as P
 
 TILE = 128
@@ -96,9 +100,470 @@
     )
 
 
+LANES = 128
+HIGHEST = lax.Precision.HIGHEST
+MESH = pl.DeviceIdType.MESH
+
+
+def dot_f32(left, right, dims):
+    return lax.dot_general(
+        left, right, (dims, ((), ())), precision=HIGHEST, preferred_element_type=jnp.float32
+    )
+
+
+def kernel(
+    line,
+    parts,
+    hidden_ref,
+    head_ref,
+    in_proj_ref,
+    out_proj_ref,
+    targets_ref,
+    lengths_ref,
+    store_ref,
+    scores_ref,
+    feat,
+    weights,
+    logits,
+    inner,
+    store,
+    table,
+    pick,
+    pick_in,
+    stat,
+    stat_in,
+    grad,
+    grad_in,
+    mix,
+    mix_in,
+    white,
+    flat,
+    load_sem,
+    head_send,
+    head_recv,
+    feat_send,
+    feat_recv,
+    pick_sems,
+    stat_sems,
+    grad_sems,
+    mix_send,
+    mix_recv,
+):
+    count = line * 4
+    me = lax.axis_index("vocab")
+    row = lax.axis_index("rows")
+    z, y, x = me // 4, (me // 2) % 2, me % 2
+    tokens, block = hidden_ref.shape
+    half = tokens // 2
+    depth, vocab_cols = head_ref.shape
+    width = out_proj_ref.shape[1]
+    own = tokens // count
+    tiles = tokens // TILE
+    seq_count = tiles * parts
+
+    def send(source, target, send_sem, recv_sem, device):
+        return pltpu.make_async_remote_copy(
+            src_ref=source,
+            dst_ref=target,
+            send_sem=send_sem,
+            recv_sem=recv_sem,
+            device_id=device,
+            device_id_type=MESH,
+        )
+
+    def await_bytes(ref, sem):
+        pltpu.make_async_copy(ref, ref, sem).wait()
+
+    barrier = pltpu.get_barrier_semaphore()
+
+    def greet(step, carry):
+        pl.semaphore_signal(
+            barrier, inc=1, device_id={"vocab": (me + step) % count}, device_id_type=MESH
+        )
+        return carry
+
+    lax.fori_loop(1, count, greet, 0)
+    for step in range(1, parts):
+        pl.semaphore_signal(
+            barrier, inc=1, device_id={"rows": (row + step) % parts}, device_id_type=MESH
+        )
+    own_rows = pl.ds(pl.multiple_of(row * depth, depth), depth)
+    local_feat = pltpu.make_async_copy(hidden_ref, feat.at[me], load_sem.at[0])
+    local_head = pltpu.make_async_copy(head_ref, weights.at[own_rows], load_sem.at[1])
+    local_store = pltpu.make_async_copy(store_ref, store, load_sem.at[2])
+    local_feat.start()
+    local_head.start()
+    local_store.start()
+    pl.semaphore_wait(barrier, count - 1 + parts - 1)
+
+    def place(zz, yy, xx):
+        return (zz * 2 + yy) * 2 + xx
+
+    def item(zz, side, pair):
+        flips = {0: (0, 0), 1: (0, 1), 2: (1, 0), 3: (1, 1)}[pair if side == 0 else (0, 2, 1, 3)[pair]]
+        return place(zz, (y + flips[0]) % 2, (x + flips[1]) % 2)
+
+    def piece(index, side):
+        return feat.at[index, pl.ds(side * half, half)]
+
+    def hop(index, side, route, device, source=None):
+        return send(
+            piece(index, side) if source is None else source,
+            piece(index, side),
+            feat_send.at[route, side, index],
+            feat_recv.at[side, index],
+            {"vocab": device},
+        )
+
+    nearest = jnp.minimum(z, line - 1 - z)
+
+    def nth(k):
+        if k == 0:
+            return z
+        sign_near = -1 if k % 2 == 1 else 1
+        sign_far = jnp.where(z < line - 1 - z, 1, -1)
+        return z + jnp.where(k <= 2 * nearest, sign_near * ((k + 1) // 2), sign_far * (k - nearest))
+
+    def outward(k, side, action):
+        zz = nth(k)
+        index = place(zz, y, x)
+        source = hidden_ref.at[pl.ds(side * half, half)] if k == 0 else None
+        up = jnp.logical_and(zz <= z, z < line - 1)
+        down = jnp.logical_and(zz >= z, z > 0)
+        if k > 0:
+            up = jnp.logical_and(zz < z, z < line - 1)
+            down = jnp.logical_and(zz > z, z > 0)
+
+        @pl.when(up)
+        def _():
+            action(hop(index, side, 0, place(jnp.minimum(z + 1, line - 1), y, x), source))
+
+        @pl.when(down)
+        def _():
+            action(hop(index, side, 1, place(jnp.maximum(z - 1, 0), y, x), source))
+
+        action(hop(index, side, 2, item(z, side, 1), source))
+        action(hop(index, side, 3, item(z, side, 2), source))
+
+    def onward(k, side):
+        return hop(item(nth(k), side, 1), side, 2, item(z, side, 2))
+
+    def arrived(index, side):
+        hop(index, side, 0, me).wait_recv()
+
+    def multiply(k):
+        zz = nth(k)
+
+        def body(step, carry):
+            side, pair = step % 2, step // 2
+            near, far = pair % 2, pair // 2
+            flip_x = (1 - side) * near + side * far
+            flip_y = (1 - side) * far + side * near
+            index = place(zz, (y + flip_y) % 2, (x + flip_x) % 2)
+
+            @pl.when(pair >= 2)
+            def _():
+                arrived(index, side)
+
+            rows = pl.ds(pl.multiple_of(side * half, half), half)
+            columns = pl.ds(pl.multiple_of(index * block, block), block)
+            features = feat[index, rows, :]
+            logits[rows, :] += jnp.dot(
+                features, weights[columns, :], preferred_element_type=jnp.float32
+            )
+            inner[rows, :] += jnp.dot(
+                features, in_proj_ref[columns, :], preferred_element_type=jnp.float32
+            )
+            return carry
+
+        lax.fori_loop(0, 8, body, 0)
+
+    for side in range(2):
+        outward(0, side, lambda copy: copy.start())
+    head_copies = []
+    for step in range(1, parts):
+        copy = send(
+            head_ref,
+            weights.at[own_rows],
+            head_send.at[step],
+            head_recv.at[row],
+            {"rows": (row + step) % parts},
+        )
+        copy.start()
+        head_copies.append(copy)
+
+    lane = lax.broadcasted_iota(jnp.int32, (vocab_cols, LANES - width), 1)
+    table[:, :width] = out_proj_ref[...]
+    table[:, width:] = (lane == 0).astype(jnp.float32).astype(jnp.bfloat16)
+    column_ids = lax.broadcasted_iota(jnp.int32, (vocab_cols, tokens), 0) + me * vocab_cols
+    onehot = (column_ids == targets_ref[...]).astype(jnp.float32).astype(jnp.bfloat16)
+    pick[...] = lax.dot_general(
+        onehot, table[...], (((0,), (0,)), ((), ())), preferred_element_type=jnp.float32
+    ).astype(jnp.bfloat16)
+
+    def own_part(ref, device):
+        return ref.at[pl.ds(pl.multiple_of(device * own, own), own)]
+
+    def slot(device):
+        return (me - device - 1 + 2 * count) % count
+
+    def send_pick(step, carry):
+        device = (me + step) % count
+        send(
+            own_part(pick, device),
+            pick_in.at[slot(device)],
+            pick_sems.at[0],
+            pick_sems.at[1],
+            {"vocab": device},
+        ).start()
+        return carry
+
+    lax.fori_loop(1, count, send_pick, 0)
+    logits[...] = jnp.zeros_like(logits)
+    inner[...] = jnp.zeros_like(inner)
+
+    for k in range(line):
+        if k > 0:
+            for side in range(2):
+                arrived(place(nth(k), y, x), side)
+                outward(k, side, lambda copy: copy.start())
+            for side in range(2):
+                arrived(item(nth(k - 1), side, 1), side)
+                onward(k - 1, side).start()
+        if k == 1:
+            local_feat.wait()
+            local_head.wait()
+            for step in range(1, parts):
+                other = (row + step) % parts
+                rows = pl.ds(pl.multiple_of(other * depth, depth), depth)
+                send(head_ref, weights.at[rows], head_send.at[0], head_recv.at[other], {"rows": row}).wait_recv()
+        if k > 1:
+            multiply(k - 2)
+    for side in range(2):
+        arrived(item(nth(line - 1), side, 1), side)
+        onward(line - 1, side).start()
+    multiply(line - 2)
+    multiply(line - 1)
+
+    lanes = lax.broadcasted_iota(jnp.int32, (TILE, LANES), 1)
+    per_tile = TILE // own
+    for tile in range(tiles):
+        part = logits[tile * TILE : (tile + 1) * TILE, :]
+        top = jnp.max(part, axis=1, keepdims=True)
+        exponent = jnp.exp(part - top)
+        upper = exponent.astype(jnp.bfloat16)
+        lower = (exponent - upper.astype(jnp.float32)).astype(jnp.bfloat16)
+        weighted = jnp.dot(upper, table[...], preferred_element_type=jnp.float32) + jnp.dot(
+            lower, table[...], preferred_element_type=jnp.float32
+        )
+        stat[tile * TILE : (tile + 1) * TILE, :] = jnp.where(lanes == width + 1, top, weighted)
+        for device in range(tile * per_tile, (tile + 1) * per_tile):
+
+            @pl.when(me != device)
+            def _():
+                send(
+                    stat.at[pl.ds(device * own, own)],
+                    stat_in.at[slot(device)],
+                    stat_sems.at[0],
+                    stat_sems.at[1],
+                    {"vocab": device},
+                ).start()
+
+    position = lax.broadcasted_iota(jnp.int32, (TILE, LANES), 0)
+    masked_in = []
+    for tile in range(tiles):
+        valid = (position < lengths_ref[row * tiles + tile]).astype(jnp.float32)
+        masked_in.append(inner[tile * TILE : (tile + 1) * TILE, :] * valid[:, :width])
+    flat_in = jnp.concatenate(masked_in, axis=0)
+    padded_in = jnp.concatenate([jnp.zeros_like(flat_in), flat_in], axis=1)
+    mix[row, tiles] = dot_f32(flat_in, padded_in, ((0,), (0,)))
+
+    await_bytes(pick_in, pick_sems.at[1])
+    picked = own_part(pick, me)[...].astype(jnp.float32)
+    for other in range(count - 1):
+        picked = picked + pick_in[other].astype(jnp.float32)
+    await_bytes(stat_in, stat_sems.at[1])
+    mine = own_part(stat, me)[...]
+    tops = [mine[:, width + 1 : width + 2]]
+    for other in range(count - 1):
+        tops.append(stat_in[other][:, width + 1 : width + 2])
+    joint = functools.reduce(jnp.maximum, tops)
+    total = mine * jnp.exp(tops[0] - joint)
+    for other in range(count - 1):
+        total = total + stat_in[other] * jnp.exp(tops[other + 1] - joint)
+    first = me * own
+    place_in_tile = lax.broadcasted_iota(jnp.int32, (own, LANES), 0) + first % TILE
+    valid = (place_in_tile < lengths_ref[row * tiles + first // TILE]).astype(jnp.float32)
+    finished = (total / total[:, width : width + 1] - picked) * valid
+    grad[...] = jnp.concatenate([finished[: own // 2, :width], finished[own // 2 :, :width]], axis=1)
+
+    def send_grad(step, carry):
+        device = (me + step) % count
+        send(grad, grad_in.at[me], grad_sems.at[0], grad_sems.at[1], {"vocab": device}).start()
+        return carry
+
+    lax.fori_loop(1, count, send_grad, 0)
+    grad_in[me] = grad[...]
+    await_bytes(grad_in.at[pl.ds(0, count - 1)], grad_sems.at[1])
+
+    for tile in range(tiles):
+        pieces = []
+        for other in range(tile * per_tile, (tile + 1) * per_tile):
+            pieces += [grad_in[other][:, :width], grad_in[other][:, width:]]
+        grads = jnp.concatenate(pieces, axis=0)
+        joined_sides = jnp.concatenate([grads, masked_in[tile]], axis=1)
+        mix[row, tile] = dot_f32(grads, joined_sides, ((0,), (0,)))
+    mix_copies = []
+    for step in range(1, parts):
+        copy = send(
+            mix.at[row], mix_in.at[row], mix_send.at[step], mix_recv.at[row], {"rows": (row + step) % parts}
+        )
+        copy.start()
+        mix_copies.append(copy)
+    mix_in[row] = mix[row]
+    for step in range(1, parts):
+        other = (row + step) % parts
+        send(mix.at[row], mix_in.at[other], mix_send.at[0], mix_recv.at[other], {"rows": row}).wait_recv()
+
+    row_total = lengths_ref[0]
+    for sequence in range(1, seq_count):
+        row_total = row_total + lengths_ref[sequence]
+    one_over = 1.0 / jnp.full((1, LANES), row_total, jnp.int32).astype(jnp.float32)
+    cov_out = jnp.zeros((width, LANES), jnp.float32)
+    cov_in = jnp.zeros((width, LANES), jnp.float32)
+    for part in range(parts):
+        for tile in range(tiles):
+            cov_out = cov_out + mix_in[part, tile]
+        cov_in = cov_in + mix_in[part, tiles]
+    left = lax.broadcasted_iota(jnp.int32, (width, LANES), 1) < width
+    cov = jnp.concatenate([jnp.where(left, cov_out, 0.0), cov_in], axis=0) * one_over
+    identity = (
+        lax.broadcasted_iota(jnp.int32, (LANES, LANES), 0)
+        == lax.broadcasted_iota(jnp.int32, (LANES, LANES), 1)
+    ).astype(jnp.float32)
+    diagonal = jnp.sum(cov * identity, axis=0, keepdims=True)
+    left_row = lax.broadcasted_iota(jnp.int32, (1, LANES), 1) < width
+    trace_out = jnp.sum(jnp.where(left_row, diagonal, 0.0), axis=1, keepdims=True)
+    trace_in = jnp.sum(jnp.where(left_row, 0.0, diagonal), axis=1, keepdims=True)
+    trace = jnp.where(left_row, trace_out, trace_in)
+    damp = damping_ratio * trace / width + tiny_value
+    middle = damp + 0.5 * trace
+    scaled = (cov + identity * damp) * (1.0 / middle)
+    reach = 1.0 / (1.0 + 2.0 * damping_ratio / width)
+    gain = 2.0 / (2.0 - reach * reach)
+    inverse = gain * (2.0 * identity - scaled)
+    reach = reach * reach / (2.0 - reach * reach)
+    while reach > 1e-8:
+        gain = 2.0 / (2.0 - reach * reach)
+        again = dot_f32(scaled, inverse, ((1,), (0,)))
+        inverse = gain * (2.0 * inverse - dot_f32(inverse, again, ((1,), (0,))))
+        reach = reach * reach / (2.0 - reach * reach)
+    inverse = inverse * (1.0 / middle)
+    stacked = []
+    for part in range(parts):
+        for tile in range(tiles):
+            long = jnp.full((1, LANES), lengths_ref[part * tiles + tile], jnp.int32)
+            stacked.append(mix_in[part, tile] * lax.rsqrt(long.astype(jnp.float32)))
+    right = dot_f32(jnp.concatenate(stacked, axis=0), inverse, ((1,), (0,)))
+    corner = inverse[:width, :width]
+    for sequence in range(seq_count):
+        rows = slice(sequence * width, (sequence + 1) * width)
+        white[rows, :] = dot_f32(corner, right[rows, :], ((1,), (0,)))
+    for pair in range(width // 2):
+        even = white[pl.ds(2 * pair, seq_count, stride=width), :]
+        odd = white[pl.ds(2 * pair + 1, seq_count, stride=width), :]
+        flat[:, pair * LANES : (pair + 1) * LANES] = jnp.concatenate(
+            [even[:, width:], odd[:, width:]], axis=1
+        )
+    local_store.wait()
+    scores_ref[...] = lax.dot_general(
+        flat[...].astype(jnp.bfloat16),
+        store[...],
+        (((1,), (1,)), ((), ())),
+        preferred_element_type=jnp.float32,
+    )
+
+    for k in range(line):
+        for side in range(2):
+            outward(k, side, lambda copy: copy.wait_send())
+            onward(k, side).wait_send()
+    for copy in head_copies + mix_copies:
+        copy.wait_send()
+    await_bytes(pick_in, pick_sems.at[0])
+    await_bytes(stat_in, stat_sems.at[0])
+    await_bytes(grad_in.at[pl.ds(0, count - 1)], grad_sems.at[0])
+
+
+def per_device_any(count, parts, hidden, head_weight, in_proj, out_proj, targets, lengths, grad_store):
+    tokens, block = hidden.shape
+    vocab_cols = head_weight.shape[1]
+    width = in_proj.shape[1]
+    own = tokens // count
+    tiles = tokens // TILE
+    fits = (
+        count % 4 == 0
+        and block % LANES == 0
+        and 2 * width == LANES
+        and own % 32 == 0
+        and TILE % own == 0
+        and grad_store.shape[1] == width * width
+    )
+    if not fits:
+        return per_device(hidden, head_weight, in_proj, out_proj, targets, lengths, grad_store)
+    line = count // 4
+    seq_count = lengths.shape[0]
+    anywhere = pl.BlockSpec(memory_space=pl.ANY)
+    vmem = pl.BlockSpec(memory_space=pltpu.VMEM)
+    smem = pl.BlockSpec(memory_space=pltpu.SMEM)
+    dma = pltpu.SemaphoreType.DMA
+    f32, bf16 = jnp.float32, jnp.bfloat16
+    return pl.pallas_call(
+        functools.partial(kernel, line, parts),
+        out_shape=jax.ShapeDtypeStruct((seq_count, grad_store.shape[0]), f32),
+        in_specs=[anywhere, anywhere, vmem, vmem, vmem, smem, anywhere],
+        out_specs=vmem,
+        scratch_shapes=[
+            pltpu.VMEM((count, tokens, block), bf16),
+            pltpu.VMEM((head_weight.shape[0] * parts, vocab_cols), bf16),
+            pltpu.VMEM((tokens, vocab_cols), f32),
+            pltpu.VMEM((tokens, width), f32),
+            pltpu.VMEM(grad_store.shape, bf16),
+            pltpu.VMEM((vocab_cols, LANES), bf16),
+            pltpu.VMEM((tokens, LANES), bf16),
+            pltpu.VMEM((count - 1, own, LANES), bf16),
+            pltpu.VMEM((tokens, LANES), f32),
+            pltpu.VMEM((count - 1, own, LANES), f32),
+            pltpu.VMEM((own // 2, LANES), f32),
+            pltpu.VMEM((count, own // 2, LANES), f32),
+            pltpu.VMEM((parts, tiles + 1, width, LANES), f32),
+            pltpu.VMEM((parts, tiles + 1, width, LANES), f32),
+            pltpu.VMEM((seq_count * width, LANES), f32),
+            pltpu.VMEM((seq_count, width * width), f32),
+            dma((3,)),
+            dma((parts,)),
+            dma((parts,)),
+            dma((4, 2, count)),
+            dma((2, count)),
+            dma((2,)),
+            dma((2,)),
+            dma((2,)),
+            dma((parts,)),
+            dma((parts,)),
+        ],
+        compiler_params=pltpu.CompilerParams(
+            collective_id=0, has_side_effects=True, vmem_limit_bytes=48 * 1024 * 1024
+        ),
+        cost_estimate=pl.CostEstimate(
+            flops=2 * tokens * block * count * vocab_cols,
+            bytes_accessed=4 * tokens * block * count,
+            transcendentals=tokens * vocab_cols,
+        ),
+    )(hidden, head_weight, in_proj, out_proj, targets[None, :], lengths, grad_store)
+
+
 def solution(mesh):
     return jax.shard_map(
-        per_device,
+        functools.partial(per_device_any, mesh.shape["vocab"], mesh.shape["rows"]),
         mesh=mesh,
         in_specs=(
             P("rows", "vocab"),

time: 347 us -> 74.5 us (0.21)
  waiting for transfers between devices: 184 us -> 0 us
  blocking collectives: 70.9 us -> 0 us
  Pallas kernels: 0 us -> 67.1 us
  other arithmetic: 44.7 us -> 0 us
  matrix products: 20.7 us -> 0 us
  between operations: 15.4 us -> 0.03 us
    all_gather x3 -> x0, waiting for transfers between devices: 111 us -> none  [the longest x1 90.6 us: per_device(): features = lax.all_gather(hidden, 'vocab', axis=1, tiled=True)]
    psum x1 -> x0, waiting for transfers between devices: 71.6 us -> none  [per_device(): picked = lax.psum(picked_local, 'vocab')]
    pallas_call x0 -> x1, Pallas kernels: none -> 67.1 us  [per_device_any(): pl.pallas_call(functools.partial(kernel, line, parts), out_shape=jax.Shap...]
    all_gather x3 -> x0, blocking collectives: 64.9 us -> none  [the longest x2 63 us: joined(): pieces = jax.tree.map(lambda part: lax.all_gather(part, axis), value)]
    another operation x10 -> x0, other arithmetic: 24.3 us -> none  [the longest x3 6.61 us: whiten(): lower_in = jnp.linalg.cholesky(cov_in + damp_in * identity)]
    dot_general x8 -> x0, matrix products: 19.4 us -> none  [the longest x1 8.3 us: per_device(): jnp.dot(features, lax.all_gather(head_weight, 'rows', axis=0, tiled=True)...]
    add x33 -> x0, other arithmetic: 18.4 us -> none  [the longest x15 18.1 us: combine_rows(): weight_one * scale_one[:, None] + weight_two * scale_two[:, None]]
    psum x1 -> x0, blocking collectives: 5.98 us -> none  [per_device(): cov_out, cov_in = lax.psum((local_out, local_in), 'rows')]
  transfers between devices with their start and end apart: 4 -> 0, of which waited for: 3 -> 0; matrix products, arithmetic and copies ran while one was open for 9% -> 0% of each run, Pallas kernels for 0% -> 0%
where the time goes in v1:
time: 74.5 us; the launch traced here: 74.2 us
  Pallas kernels  67.1 us (90%)
  local copies, waits for them, and re-layouts  7.07 us (9%)
    pallas_call x1, Pallas kernels, per_device_any(): pl.pallas_call(functools.partial(kernel, line, parts), out_shape=jax.Shap...  67.1 us
    unnamed x11, local copies, waits for them, and re-layouts  7.07 us

profile of v1, /device:TPU:1, one launch (start us, length us, event | category | flops | bytes accessed | tf_op | source)
XLA Modules:
  0.0 74.2 jit_solution(10507641665023551164)
XLA Ops:
  0.0 1.1 %copy.9.out_proj_ref = bf16[1024,64]{1,0:T(8,128)(2,1)S(1)} copy(bf16[1024,64]{0,1:T(8,128)(2,1)} %param.10) | data formatting | bytes 262144 | tf_op args[3]
  1.1 1.5 %copy.8.in_proj_ref = bf16[4096,64]{1,0:T(8,128)(2,1)S(1)} copy(bf16[4096,64]{0,1:T(8,128)(2,1)} %param.9) | data formatting | bytes 1048576 | tf_op args[2]
  2.6 0.0 copy-start
  2.6 1.6 %copy-done = bf16[256,4096]{1,0:T(8,128)(2,1)S(1)} copy-done((bf16[256,4096]{1,0:T(8,128)(2,1)S(1)}, bf16[256,4096]{1,0:T(8,128)(2,1)}, u32[]{:S(2)}) %copy-start) | copy-done | bytes 2097176
  4.2 0.0 copy-start.1
  4.2 0.9 %copy-done.1 = bf16[512,256]{1,0:T(8,128)(2,1)S(1)} copy-done((bf16[512,256]{1,0:T(8,128)(2,1)S(1)}, bf16[512,256]{1,0:T(8,128)(2,1)}, u32[]{:S(2)}) %copy-start.1) | copy-done | bytes 262168
  5.2 0.0 copy-start.2
  5.2 0.7 copy-done.2
  5.8 0.0 copy-start.3
  5.8 0.7 copy-done.3
  6.5 67.1 %shard_map.73 = f32[8,256]{1,0:T(8,128)S(1)} custom-call(bf16[512,256]{1,0:T(8,128)(2,1)S(1)} %copy-done.1, bf16[2048,1024]{1,0:T(8,128)(2,1)} %head_ref.1, bf16[4096,64]{1,0:T(8,128)(2,1)S(1)} %copy.8.in_proj_ref, bf16[1024,64]{1,0:T(8,128)(2,1)S(1)} %copy.9.out_proj_ref, s32[1,512]{1,0:T(1,128)S(1)} %bitcast.1, s32[8]{0:T(128)S(1)} %copy-done.3, ...), custom_call_target="tpu_custom_call" | custom-call | flops 4294967296 | bytes 8388608 | tf_op jit(solution)/shard_map/pallas_call | solution.py:520
  73.6 0.6 copy.11
Async XLA Ops:
  2.6 1.6 %copy-start = (bf16[256,4096]{1,0:T(8,128)(2,1)S(1)}, bf16[256,4096]{1,0:T(8,128)(2,1)}, u32[]{:S(2)}) copy-start(bf16[256,4096]{1,0:T(8,128)(2,1)} %store_ref.1) | copy-start | bytes 6291460
  4.2 0.9 %copy-start.1 = (bf16[512,256]{1,0:T(8,128)(2,1)S(1)}, bf16[512,256]{1,0:T(8,128)(2,1)}, u32[]{:S(2)}) copy-start(bf16[512,256]{1,0:T(8,128)(2,1)} %hidden_ref.1) | copy-start | bytes 786436
  5.2 0.7 copy-start.2
  5.8 0.7 copy-start.3

commit v2 on v1

--- a/solution.py
+++ b/solution.py
@@ -111,15 +111,29 @@
     )
 
 
+def split(value):
+    upper = value.astype(jnp.bfloat16)
+    return upper, (value - upper.astype(jnp.float32)).astype(jnp.bfloat16)
+
+
+def dot_three(left, right):
+    left_upper, left_lower = split(left)
+    right_upper, right_lower = split(right)
+    small = jnp.dot(left_upper, right_lower, preferred_element_type=jnp.float32) + jnp.dot(
+        left_lower, right_upper, preferred_element_type=jnp.float32
+    )
+    return small + jnp.dot(left_upper, right_upper, preferred_element_type=jnp.float32)
+
+
 def kernel(
     line,
     parts,
     hidden_ref,
     head_ref,
-    in_proj_ref,
-    out_proj_ref,
-    targets_ref,
-    lengths_ref,
+    in_proj_hbm,
+    out_proj_hbm,
+    targets_hbm,
+    lengths_hbm,
     store_ref,
     scores_ref,
     feat,
@@ -127,6 +141,10 @@
     logits,
     inner,
     store,
+    in_proj_ref,
+    out_proj_ref,
+    targets_ref,
+    lengths_ref,
     table,
     pick,
     pick_in,
@@ -154,9 +172,11 @@
     row = lax.axis_index("rows")
     z, y, x = me // 4, (me // 2) % 2, me % 2
     tokens, block = hidden_ref.shape
-    half = tokens // 2
+    long_rows, short_rows = class_rows(tokens)
+    starts = (0, long_rows, 2 * long_rows, 2 * long_rows + short_rows)
+    sizes = (long_rows, long_rows, short_rows, short_rows)
     depth, vocab_cols = head_ref.shape
-    width = out_proj_ref.shape[1]
+    width = out_proj_ref.shape[0]
     own = tokens // count
     tiles = tokens // TILE
     seq_count = tiles * parts
@@ -192,6 +212,19 @@
     local_head = pltpu.make_async_copy(head_ref, weights.at[own_rows], load_sem.at[1])
     local_store = pltpu.make_async_copy(store_ref, store, load_sem.at[2])
     local_feat.start()
+    small = [
+        pltpu.make_async_copy(source, target, load_sem.at[3 + at])
+        for at, (source, target) in enumerate(
+            [
+                (out_proj_hbm, out_proj_ref),
+                (targets_hbm, targets_ref),
+                (lengths_hbm, lengths_ref),
+                (in_proj_hbm, in_proj_ref),
+            ]
+        )
+    ]
+    for copy in small:
+        copy.start()
     local_head.start()
     local_store.start()
     pl.semaphore_wait(barrier, count - 1 + parts - 1)
@@ -200,11 +233,12 @@
         return (zz * 2 + yy) * 2 + xx
 
     def item(zz, side, pair):
-        flips = {0: (0, 0), 1: (0, 1), 2: (1, 0), 3: (1, 1)}[pair if side == 0 else (0, 2, 1, 3)[pair]]
-        return place(zz, (y + flips[0]) % 2, (x + flips[1]) % 2)
+        near, far = pair % 2, pair // 2
+        flip_y, flip_x = (far, near) if side % 2 == 0 else (near, far)
+        return place(zz, (y + flip_y) % 2, (x + flip_x) % 2)
 
     def piece(index, side):
-        return feat.at[index, pl.ds(side * half, half)]
+        return feat.at[index, pl.ds(starts[side], sizes[side])]
 
     def hop(index, side, route, device, source=None):
         return send(
@@ -224,15 +258,17 @@
         sign_far = jnp.where(z < line - 1 - z, 1, -1)
         return z + jnp.where(k <= 2 * nearest, sign_near * ((k + 1) // 2), sign_far * (k - nearest))
 
-    def outward(k, side, action):
+    def own_rows_of(side):
+        return hidden_ref.at[pl.ds(starts[side], sizes[side])]
+
+    def along(k, side, pair, action, source=None):
         zz = nth(k)
-        index = place(zz, y, x)
-        source = hidden_ref.at[pl.ds(side * half, half)] if k == 0 else None
-        up = jnp.logical_and(zz <= z, z < line - 1)
-        down = jnp.logical_and(zz >= z, z > 0)
+        index = item(zz, side, pair)
+        up = z < line - 1
+        down = z > 0
         if k > 0:
-            up = jnp.logical_and(zz < z, z < line - 1)
-            down = jnp.logical_and(zz > z, z > 0)
+            up = jnp.logical_and(zz < z, up)
+            down = jnp.logical_and(zz > z, down)
 
         @pl.when(up)
         def _():
@@ -242,6 +278,10 @@
         def _():
             action(hop(index, side, 1, place(jnp.maximum(z - 1, 0), y, x), source))
 
+    def outward(k, side, action):
+        source = own_rows_of(side) if k == 0 else None
+        index = item(nth(k), side, 0)
+        along(k, side, 0, action, source)
         action(hop(index, side, 2, item(z, side, 1), source))
         action(hop(index, side, 3, item(z, side, 2), source))
 
@@ -250,6 +290,20 @@
 
     def arrived(index, side):
         hop(index, side, 0, me).wait_recv()
+
+    def accumulate(index, start, size):
+        rows = pl.ds(pl.multiple_of(start, 16), size)
+        columns = pl.ds(pl.multiple_of(index * block, block), block)
+        features = feat[index, rows, :]
+        logits[rows, :] += jnp.dot(
+            features, weights[columns, :], preferred_element_type=jnp.float32
+        )
+        inner[rows, :] += lax.dot_general(
+            features,
+            in_proj_ref[:, columns],
+            (((1,), (1,)), ((), ())),
+            preferred_element_type=jnp.float32,
+        )
 
     def multiply(k):
         zz = nth(k)
@@ -263,21 +317,46 @@
 
             @pl.when(pair >= 2)
             def _():
-                arrived(index, side)
-
-            rows = pl.ds(pl.multiple_of(side * half, half), half)
-            columns = pl.ds(pl.multiple_of(index * block, block), block)
-            features = feat[index, rows, :]
-            logits[rows, :] += jnp.dot(
-                features, weights[columns, :], preferred_element_type=jnp.float32
-            )
-            inner[rows, :] += jnp.dot(
-                features, in_proj_ref[columns, :], preferred_element_type=jnp.float32
-            )
+                pltpu.make_async_copy(
+                    piece(index, 0), piece(index, 0), feat_recv.at[side, index]
+                ).wait()
+
+            accumulate(index, side * long_rows, long_rows)
             return carry
 
         lax.fori_loop(0, 8, body, 0)
 
+    def multiply_short(k):
+        zz = nth(k)
+
+        def body(pair, carry):
+            index = place(zz, (y + pair // 2) % 2, (x + pair % 2) % 2)
+            accumulate(index, 2 * long_rows, 2 * short_rows)
+            return carry
+
+        lax.fori_loop(0, 4, body, 0)
+
+    def short_arrivals(k):
+        for pair in range(4):
+            for side in (2, 3):
+                if k > 0:
+                    arrived(item(nth(k), side, pair), side)
+                    along(k, side, pair, lambda copy: copy.start())
+
+    def short_start(side, action):
+        source = own_rows_of(side)
+        action(hop(me, side, 2, item(z, side, 1), source))
+        action(hop(me, side, 3, item(z, side, 2), source))
+        along(0, side, 0, action, source)
+
+    def short_onward(pair, side, action):
+        index = item(z, side, pair)
+        if pair == 1:
+            action(hop(index, side, 2, item(z, side, 2)))
+        along(0, side, pair, action)
+
+    for side in (2, 3):
+        short_start(side, lambda copy: copy.start())
     for side in range(2):
         outward(0, side, lambda copy: copy.start())
     head_copies = []
@@ -292,14 +371,16 @@
         copy.start()
         head_copies.append(copy)
 
-    lane = lax.broadcasted_iota(jnp.int32, (vocab_cols, LANES - width), 1)
-    table[:, :width] = out_proj_ref[...]
-    table[:, width:] = (lane == 0).astype(jnp.float32).astype(jnp.bfloat16)
+    for copy in small:
+        copy.wait()
+    marker = lax.broadcasted_iota(jnp.int32, (LANES - width, vocab_cols), 0)
+    upright = jnp.concatenate([out_proj_ref[...].astype(jnp.float32), (marker == 0).astype(jnp.float32)], axis=0)
+    table[...] = upright.T.astype(jnp.bfloat16)
     column_ids = lax.broadcasted_iota(jnp.int32, (vocab_cols, tokens), 0) + me * vocab_cols
     onehot = (column_ids == targets_ref[...]).astype(jnp.float32).astype(jnp.bfloat16)
-    pick[...] = lax.dot_general(
-        onehot, table[...], (((0,), (0,)), ((), ())), preferred_element_type=jnp.float32
-    ).astype(jnp.bfloat16)
+    pick[...] = jnp.dot(
+        upright.astype(jnp.bfloat16), onehot, preferred_element_type=jnp.float32
+    ).T.astype(jnp.bfloat16)
 
     def own_part(ref, device):
         return ref.at[pl.ds(pl.multiple_of(device * own, own), own)]
@@ -323,6 +404,11 @@
     inner[...] = jnp.zeros_like(inner)
 
     for k in range(line):
+        if k == 1:
+            for pair in (1, 2, 3):
+                for side in (2, 3):
+                    arrived(item(z, side, pair), side)
+                    short_onward(pair, side, lambda copy: copy.start())
         if k > 0:
             for side in range(2):
                 arrived(place(nth(k), y, x), side)
@@ -330,6 +416,7 @@
             for side in range(2):
                 arrived(item(nth(k - 1), side, 1), side)
                 onward(k - 1, side).start()
+            short_arrivals(k - 1)
         if k == 1:
             local_feat.wait()
             local_head.wait()
@@ -339,10 +426,14 @@
                 send(head_ref, weights.at[rows], head_send.at[0], head_recv.at[other], {"rows": row}).wait_recv()
         if k > 1:
             multiply(k - 2)
+            multiply_short(k - 2)
     for side in range(2):
         arrived(item(nth(line - 1), side, 1), side)
         onward(line - 1, side).start()
     multiply(line - 2)
+    multiply_short(line - 2)
+    short_arrivals(line - 1)
+    multiply_short(line - 1)
     multiply(line - 1)
 
     lanes = lax.broadcasted_iota(jnp.int32, (TILE, LANES), 1)
@@ -455,20 +546,23 @@
     reach = reach * reach / (2.0 - reach * reach)
     while reach > 1e-8:
         gain = 2.0 / (2.0 - reach * reach)
-        again = dot_f32(scaled, inverse, ((1,), (0,)))
-        inverse = gain * (2.0 * inverse - dot_f32(inverse, again, ((1,), (0,))))
         reach = reach * reach / (2.0 - reach * reach)
+        if reach > 1e-3:
+            inverse = gain * (2.0 * inverse - dot_three(inverse, dot_three(scaled, inverse)))
+        else:
+            again = dot_f32(scaled, inverse, ((1,), (0,)))
+            inverse = gain * (2.0 * inverse - dot_f32(inverse, again, ((1,), (0,))))
     inverse = inverse * (1.0 / middle)
     stacked = []
     for part in range(parts):
         for tile in range(tiles):
             long = jnp.full((1, LANES), lengths_ref[part * tiles + tile], jnp.int32)
             stacked.append(mix_in[part, tile] * lax.rsqrt(long.astype(jnp.float32)))
-    right = dot_f32(jnp.concatenate(stacked, axis=0), inverse, ((1,), (0,)))
+    right = dot_three(jnp.concatenate(stacked, axis=0), inverse)
     corner = inverse[:width, :width]
     for sequence in range(seq_count):
         rows = slice(sequence * width, (sequence + 1) * width)
-        white[rows, :] = dot_f32(corner, right[rows, :], ((1,), (0,)))
+        white[rows, :] = dot_three(corner, right[rows, :])
     for pair in range(width // 2):
         even = white[pl.ds(2 * pair, seq_count, stride=width), :]
         odd = white[pl.ds(2 * pair + 1, seq_count, stride=width), :]
@@ -487,11 +581,24 @@
         for side in range(2):
             outward(k, side, lambda copy: copy.wait_send())
             onward(k, side).wait_send()
+        for side in (2, 3):
+            for pair in range(4):
+                if k > 0:
+                    along(k, side, pair, lambda copy: copy.wait_send())
+                elif pair > 0:
+                    short_onward(pair, side, lambda copy: copy.wait_send())
+                else:
+                    short_start(side, lambda copy: copy.wait_send())
     for copy in head_copies + mix_copies:
         copy.wait_send()
     await_bytes(pick_in, pick_sems.at[0])
     await_bytes(stat_in, stat_sems.at[0])
     await_bytes(grad_in.at[pl.ds(0, count - 1)], grad_sems.at[0])
+
+
+def class_rows(tokens):
+    short = tokens // 10 // 16 * 16
+    return tokens // 2 - short, short
 
 
 def per_device_any(count, parts, hidden, head_weight, in_proj, out_proj, targets, lengths, grad_store):
@@ -505,6 +612,8 @@
         and block % LANES == 0
         and 2 * width == LANES
         and own % 32 == 0
+        and tokens % 32 == 0
+        and tokens >= 160
         and TILE % own == 0
         and grad_store.shape[1] == width * width
     )
@@ -512,15 +621,14 @@
         return per_device(hidden, head_weight, in_proj, out_proj, targets, lengths, grad_store)
     line = count // 4
     seq_count = lengths.shape[0]
-    anywhere = pl.BlockSpec(memory_space=pl.ANY)
+    hbm = pl.BlockSpec(memory_space=pltpu.HBM)
     vmem = pl.BlockSpec(memory_space=pltpu.VMEM)
-    smem = pl.BlockSpec(memory_space=pltpu.SMEM)
     dma = pltpu.SemaphoreType.DMA
     f32, bf16 = jnp.float32, jnp.bfloat16
     return pl.pallas_call(
         functools.partial(kernel, line, parts),
         out_shape=jax.ShapeDtypeStruct((seq_count, grad_store.shape[0]), f32),
-        in_specs=[anywhere, anywhere, vmem, vmem, vmem, smem, anywhere],
+        in_specs=[hbm] * 7,
         out_specs=vmem,
         scratch_shapes=[
             pltpu.VMEM((count, tokens, block), bf16),
@@ -528,6 +636,10 @@
             pltpu.VMEM((tokens, vocab_cols), f32),
             pltpu.VMEM((tokens, width), f32),
             pltpu.VMEM(grad_store.shape, bf16),
+            pltpu.VMEM(in_proj.shape[::-1], bf16),
+            pltpu.VMEM(out_proj.shape[::-1], bf16),
+            pltpu.VMEM((1, tokens), jnp.int32),
+            pltpu.SMEM(lengths.shape, jnp.int32),
             pltpu.VMEM((vocab_cols, LANES), bf16),
             pltpu.VMEM((tokens, LANES), bf16),
             pltpu.VMEM((count - 1, own, LANES), bf16),
@@ -539,11 +651,11 @@
             pltpu.VMEM((parts, tiles + 1, width, LANES), f32),
             pltpu.VMEM((seq_count * width, LANES), f32),
             pltpu.VMEM((seq_count, width * width), f32),
-            dma((3,)),
+            dma((7,)),
             dma((parts,)),
             dma((parts,)),
-            dma((4, 2, count)),
-            dma((2, count)),
+            dma((4, 4, count)),
+            dma((4, count)),
             dma((2,)),
             dma((2,)),
             dma((2,)),
@@ -551,14 +663,14 @@
             dma((parts,)),
         ],
         compiler_params=pltpu.CompilerParams(
-            collective_id=0, has_side_effects=True, vmem_limit_bytes=48 * 1024 * 1024
+            collective_id=0, has_side_effects=True, vmem_limit_bytes=64 * 1024 * 1024
         ),
         cost_estimate=pl.CostEstimate(
             flops=2 * tokens * block * count * vocab_cols,
             bytes_accessed=4 * tokens * block * count,
             transcendentals=tokens * vocab_cols,
         ),
-    )(hidden, head_weight, in_proj, out_proj, targets[None, :], lengths, grad_store)
+    )(hidden, head_weight, in_proj.T, out_proj.T, targets[None, :], lengths, grad_store)
 
 
 def solution(mesh):

time: 74.5 us -> 71.9 us (0.965)
  local copies, waits for them, and re-layouts: 7.07 us -> 1.3 us
  Pallas kernels: 67.1 us -> 70.4 us
    unnamed x11 -> x1, local copies, waits for them, and re-layouts: 7.07 us -> 1.3 us
    pallas_call x1, Pallas kernels: 67.1 us -> 70.4 us  [per_device_any(): pl.pallas_call(functools.partial(kernel, line, parts), out_shape=jax.Shap...]
where the time goes in v2:
time: 71.9 us; the launch traced here: 71.7 us
  Pallas kernels  70.4 us (98%)
  local copies, waits for them, and re-layouts  1.3 us (2%)
    pallas_call x1, Pallas kernels, per_device_any(): pl.pallas_call(functools.partial(kernel, line, parts), out_shape=jax.Shap...  70.4 us

profile of v2, /device:TPU:1, one launch (start us, length us, event | category | flops | bytes accessed | tf_op | source)
XLA Modules:
  0.0 71.7 jit_solution(11616978822255639020)
XLA Ops:
  0.0 70.4 %shard_map.73 = f32[8,256]{1,0:T(8,128)} custom-call(bf16[512,256]{1,0:T(8,128)(2,1)} %hidden_ref.1, bf16[2048,1024]{1,0:T(8,128)(2,1)} %head_ref.1, bf16[64,4096]{1,0:T(8,128)(2,1)} %bitcast.3, bf16[64,1024]{1,0:T(8,128)(2,1)} %bitcast.4, s32[1,512]{1,0:T(1,128)} %bitcast.5, s32[8]{0:T(128)} %lengths_hbm.1, bf16[256,4096]{1,0:T(8,128)(2,1)} %store_ref.1), custom_call_target="tpu_custom_call" | custom-call | flops 4294967296 | bytes 8388608 | tf_op jit(solution)/shard_map/pallas_call | solution.py:628
  70.4 1.3 %copy.9 = f32[8,256]{1,0:T(8,128)} copy(f32[8,256]{1,0:T(8,128)} %shard_map.73) | data formatting | bytes 16384

commit v3 on v2

--- a/solution.py
+++ b/solution.py
@@ -123,6 +123,31 @@
         left_lower, right_upper, preferred_element_type=jnp.float32
     )
     return small + jnp.dot(left_upper, right_upper, preferred_element_type=jnp.float32)
+
+
+def damped_inverse(cov):
+    width = cov.shape[0]
+    identity = (
+        lax.broadcasted_iota(jnp.int32, cov.shape, 0) == lax.broadcasted_iota(jnp.int32, cov.shape, 1)
+    ).astype(jnp.float32)
+    diagonal = jnp.sum(cov * identity, axis=0, keepdims=True)
+    trace = jnp.sum(diagonal, axis=1, keepdims=True)
+    damp = damping_ratio * trace / width + tiny_value
+    shrink = 1.0 / (damp + 0.5 * trace)
+    scaled = (cov + identity * damp) * shrink
+    reach = 1.0 / (1.0 + 2.0 * damping_ratio / width)
+    gain = 2.0 / (2.0 - reach * reach)
+    inverse = gain * (2.0 * identity - scaled)
+    reach = reach * reach / (2.0 - reach * reach)
+    while reach > 1e-8:
+        gain = 2.0 / (2.0 - reach * reach)
+        reach = reach * reach / (2.0 - reach * reach)
+        if reach > 1e-3:
+            inverse = gain * (2.0 * inverse - dot_three(inverse, dot_three(scaled, inverse)))
+        else:
+            again = dot_f32(scaled, inverse, ((1,), (0,)))
+            inverse = gain * (2.0 * inverse - dot_f32(inverse, again, ((1,), (0,))))
+    return inverse * shrink
 
 
 def kernel(
@@ -152,6 +177,7 @@
     stat_in,
     grad,
     grad_in,
+    side_in,
     mix,
     mix_in,
     white,
@@ -164,6 +190,8 @@
     pick_sems,
     stat_sems,
     grad_sems,
+    side_send,
+    side_recv,
     mix_send,
     mix_recv,
 ):
@@ -207,9 +235,7 @@
         pl.semaphore_signal(
             barrier, inc=1, device_id={"rows": (row + step) % parts}, device_id_type=MESH
         )
-    own_rows = pl.ds(pl.multiple_of(row * depth, depth), depth)
     local_feat = pltpu.make_async_copy(hidden_ref, feat.at[me], load_sem.at[0])
-    local_head = pltpu.make_async_copy(head_ref, weights.at[own_rows], load_sem.at[1])
     local_store = pltpu.make_async_copy(store_ref, store, load_sem.at[2])
     local_feat.start()
     small = [
@@ -225,7 +251,18 @@
     ]
     for copy in small:
         copy.start()
-    local_head.start()
+    chunk = 4 * block
+    per_part = line // parts
+
+    def head_chunk(zz):
+        return weights.at[pl.ds(pl.multiple_of(zz * chunk, chunk), chunk)]
+
+    for at in range(per_part):
+        pltpu.make_async_copy(
+            head_ref.at[pl.ds(at * chunk, chunk)],
+            head_chunk(row * per_part + at),
+            head_recv.at[row * per_part + at],
+        ).start()
     local_store.start()
     pl.semaphore_wait(barrier, count - 1 + parts - 1)
 
@@ -307,6 +344,7 @@
 
     def multiply(k):
         zz = nth(k)
+        pltpu.make_async_copy(head_chunk(zz), head_chunk(zz), head_recv.at[zz]).wait()
 
         def body(step, carry):
             side, pair = step % 2, step // 2
@@ -359,17 +397,26 @@
         short_start(side, lambda copy: copy.start())
     for side in range(2):
         outward(0, side, lambda copy: copy.start())
-    head_copies = []
-    for step in range(1, parts):
-        copy = send(
-            head_ref,
-            weights.at[own_rows],
-            head_send.at[step],
-            head_recv.at[row],
+    def head_copy(k, step):
+        zz = nth(k)
+        at = zz % per_part
+        return send(
+            head_ref.at[pl.ds(pl.multiple_of(at * chunk, chunk), chunk)],
+            head_chunk(zz),
+            head_send.at[step, zz],
+            head_recv.at[zz],
             {"rows": (row + step) % parts},
         )
-        copy.start()
-        head_copies.append(copy)
+
+    def head_sends(action):
+        for k in range(line):
+
+            @pl.when(nth(k) // per_part == row)
+            def _():
+                for step in range(1, parts):
+                    action(head_copy(k, step))
+
+    head_sends(lambda copy: copy.start())
 
     for copy in small:
         copy.wait()
@@ -419,11 +466,6 @@
             short_arrivals(k - 1)
         if k == 1:
             local_feat.wait()
-            local_head.wait()
-            for step in range(1, parts):
-                other = (row + step) % parts
-                rows = pl.ds(pl.multiple_of(other * depth, depth), depth)
-                send(head_ref, weights.at[rows], head_send.at[0], head_recv.at[other], {"rows": row}).wait_recv()
         if k > 1:
             multiply(k - 2)
             multiply_short(k - 2)
@@ -433,8 +475,8 @@
     multiply(line - 2)
     multiply_short(line - 2)
     short_arrivals(line - 1)
+    multiply(line - 1)
     multiply_short(line - 1)
-    multiply(line - 1)
 
     lanes = lax.broadcasted_iota(jnp.int32, (TILE, LANES), 1)
     per_tile = TILE // own
@@ -466,8 +508,39 @@
         valid = (position < lengths_ref[row * tiles + tile]).astype(jnp.float32)
         masked_in.append(inner[tile * TILE : (tile + 1) * TILE, :] * valid[:, :width])
     flat_in = jnp.concatenate(masked_in, axis=0)
-    padded_in = jnp.concatenate([jnp.zeros_like(flat_in), flat_in], axis=1)
-    mix[row, tiles] = dot_f32(flat_in, padded_in, ((0,), (0,)))
+    side_in[row] = dot_f32(flat_in, flat_in, ((0,), (0,)))
+    side_copies = []
+    for step in range(1, parts):
+        copy = send(
+            side_in.at[row], side_in.at[row], side_send.at[step], side_recv.at[row], {"rows": (row + step) % parts}
+        )
+        copy.start()
+        side_copies.append(copy)
+    row_total = lengths_ref[0]
+    for sequence in range(1, seq_count):
+        row_total = row_total + lengths_ref[sequence]
+    one_over = 1.0 / jnp.full((1, width), row_total, jnp.int32).astype(jnp.float32)
+    for k in range(line):
+        for side in range(2):
+            outward(k, side, lambda copy: copy.wait_send())
+            onward(k, side).wait_send()
+        for side in (2, 3):
+            for pair in range(4):
+                if k > 0:
+                    along(k, side, pair, lambda copy: copy.wait_send())
+                elif pair > 0:
+                    short_onward(pair, side, lambda copy: copy.wait_send())
+                else:
+                    short_start(side, lambda copy: copy.wait_send())
+    head_sends(lambda copy: copy.wait_send())
+    for step in range(1, parts):
+        other = (row + step) % parts
+        send(side_in.at[row], side_in.at[other], side_send.at[0], side_recv.at[other], {"rows": row}).wait_recv()
+    cov_in = side_in[0]
+    for part in range(1, parts):
+        cov_in = cov_in + side_in[part]
+    inverse_in = damped_inverse(cov_in * one_over)
+    flat_in = dot_three(flat_in, inverse_in)
 
     await_bytes(pick_in, pick_sems.at[1])
     picked = own_part(pick, me)[...].astype(jnp.float32)
@@ -502,7 +575,7 @@
         for other in range(tile * per_tile, (tile + 1) * per_tile):
             pieces += [grad_in[other][:, :width], grad_in[other][:, width:]]
         grads = jnp.concatenate(pieces, axis=0)
-        joined_sides = jnp.concatenate([grads, masked_in[tile]], axis=1)
+        joined_sides = jnp.concatenate([grads, flat_in[tile * TILE : (tile + 1) * TILE, :]], axis=1)
         mix[row, tile] = dot_f32(grads, joined_sides, ((0,), (0,)))
     mix_copies = []
     for step in range(1, parts):
@@ -516,53 +589,20 @@
         other = (row + step) % parts
         send(mix.at[row], mix_in.at[other], mix_send.at[0], mix_recv.at[other], {"rows": row}).wait_recv()
 
-    row_total = lengths_ref[0]
-    for sequence in range(1, seq_count):
-        row_total = row_total + lengths_ref[sequence]
-    one_over = 1.0 / jnp.full((1, LANES), row_total, jnp.int32).astype(jnp.float32)
     cov_out = jnp.zeros((width, LANES), jnp.float32)
-    cov_in = jnp.zeros((width, LANES), jnp.float32)
-    for part in range(parts):
-        for tile in range(tiles):
-            cov_out = cov_out + mix_in[part, tile]
-        cov_in = cov_in + mix_in[part, tiles]
-    left = lax.broadcasted_iota(jnp.int32, (width, LANES), 1) < width
-    cov = jnp.concatenate([jnp.where(left, cov_out, 0.0), cov_in], axis=0) * one_over
-    identity = (
-        lax.broadcasted_iota(jnp.int32, (LANES, LANES), 0)
-        == lax.broadcasted_iota(jnp.int32, (LANES, LANES), 1)
-    ).astype(jnp.float32)
-    diagonal = jnp.sum(cov * identity, axis=0, keepdims=True)
-    left_row = lax.broadcasted_iota(jnp.int32, (1, LANES), 1) < width
-    trace_out = jnp.sum(jnp.where(left_row, diagonal, 0.0), axis=1, keepdims=True)
-    trace_in = jnp.sum(jnp.where(left_row, 0.0, diagonal), axis=1, keepdims=True)
-    trace = jnp.where(left_row, trace_out, trace_in)
-    damp = damping_ratio * trace / width + tiny_value
-    middle = damp + 0.5 * trace
-    scaled = (cov + identity * damp) * (1.0 / middle)
-    reach = 1.0 / (1.0 + 2.0 * damping_ratio / width)
-    gain = 2.0 / (2.0 - reach * reach)
-    inverse = gain * (2.0 * identity - scaled)
-    reach = reach * reach / (2.0 - reach * reach)
-    while reach > 1e-8:
-        gain = 2.0 / (2.0 - reach * reach)
-        reach = reach * reach / (2.0 - reach * reach)
-        if reach > 1e-3:
-            inverse = gain * (2.0 * inverse - dot_three(inverse, dot_three(scaled, inverse)))
-        else:
-            again = dot_f32(scaled, inverse, ((1,), (0,)))
-            inverse = gain * (2.0 * inverse - dot_f32(inverse, again, ((1,), (0,))))
-    inverse = inverse * (1.0 / middle)
     stacked = []
     for part in range(parts):
         for tile in range(tiles):
+            block_mix = mix_in[part, tile]
+            cov_out = cov_out + block_mix
             long = jnp.full((1, LANES), lengths_ref[part * tiles + tile], jnp.int32)
-            stacked.append(mix_in[part, tile] * lax.rsqrt(long.astype(jnp.float32)))
-    right = dot_three(jnp.concatenate(stacked, axis=0), inverse)
-    corner = inverse[:width, :width]
+            stacked.append(block_mix * lax.rsqrt(long.astype(jnp.float32)))
+    inverse_out = damped_inverse(cov_out[:, :width] * one_over)
+    whitened = dot_three(inverse_out, jnp.concatenate(stacked, axis=1))
     for sequence in range(seq_count):
-        rows = slice(sequence * width, (sequence + 1) * width)
-        white[rows, :] = dot_three(corner, right[rows, :])
+        white[sequence * width : (sequence + 1) * width, :] = whitened[
+            :, sequence * LANES : (sequence + 1) * LANES
+        ]
     for pair in range(width // 2):
         even = white[pl.ds(2 * pair, seq_count, stride=width), :]
         odd = white[pl.ds(2 * pair + 1, seq_count, stride=width), :]
@@ -577,19 +617,7 @@
         preferred_element_type=jnp.float32,
     )
 
-    for k in range(line):
-        for side in range(2):
-            outward(k, side, lambda copy: copy.wait_send())
-            onward(k, side).wait_send()
-        for side in (2, 3):
-            for pair in range(4):
-                if k > 0:
-                    along(k, side, pair, lambda copy: copy.wait_send())
-                elif pair > 0:
-                    short_onward(pair, side, lambda copy: copy.wait_send())
-                else:
-                    short_start(side, lambda copy: copy.wait_send())
-    for copy in head_copies + mix_copies:
+    for copy in side_copies + mix_copies:
         copy.wait_send()
     await_bytes(pick_in, pick_sems.at[0])
     await_bytes(stat_in, stat_sems.at[0])
@@ -608,7 +636,7 @@
     own = tokens // count
     tiles = tokens // TILE
     fits = (
-        count % 4 == 0
+        count % (4 * parts) == 0
         and block % LANES == 0
         and 2 * width == LANES
         and own % 32 == 0
@@ -647,18 +675,21 @@
             pltpu.VMEM((count - 1, own, LANES), f32),
             pltpu.VMEM((own // 2, LANES), f32),
             pltpu.VMEM((count, own // 2, LANES), f32),
-            pltpu.VMEM((parts, tiles + 1, width, LANES), f32),
-            pltpu.VMEM((parts, tiles + 1, width, LANES), f32),
+            pltpu.VMEM((parts, width, width), f32),
+            pltpu.VMEM((parts, tiles, width, LANES), f32),
+            pltpu.VMEM((parts, tiles, width, LANES), f32),
             pltpu.VMEM((seq_count * width, LANES), f32),
             pltpu.VMEM((seq_count, width * width), f32),
             dma((7,)),
-            dma((parts,)),
-            dma((parts,)),
+            dma((parts, line)),
+            dma((line,)),
             dma((4, 4, count)),
             dma((4, count)),
             dma((2,)),
             dma((2,)),
             dma((2,)),
+            dma((parts,)),
+            dma((parts,)),
             dma((parts,)),
             dma((parts,)),
         ],

time: 71.9 us -> 71 us (0.987)
  Pallas kernels: 70.4 us -> 69.5 us
    pallas_call x1, Pallas kernels: 70.4 us -> 69.5 us  [per_device_any(): pl.pallas_call(functools.partial(kernel, line, parts), out_shape=jax.Shap...]
where the time goes in v3:
time: 71 us; the launch traced here: 70.8 us
  Pallas kernels  69.5 us (98%)
  local copies, waits for them, and re-layouts  1.3 us (2%)
    pallas_call x1, Pallas kernels, per_device_any(): pl.pallas_call(functools.partial(kernel, line, parts), out_shape=jax.Shap...  69.5 us

profile of v3, /device:TPU:1, one launch (start us, length us, event | category | flops | bytes accessed | tf_op | source)
XLA Modules:
  0.0 70.8 jit_solution(1081682498381383199)
XLA Ops:
  0.0 69.5 %shard_map.73 = f32[8,256]{1,0:T(8,128)} custom-call(bf16[512,256]{1,0:T(8,128)(2,1)} %hidden_ref.1, bf16[2048,1024]{1,0:T(8,128)(2,1)} %head_ref.1, bf16[64,4096]{1,0:T(8,128)(2,1)} %bitcast.3, bf16[64,1024]{1,0:T(8,128)(2,1)} %bitcast.4, s32[1,512]{1,0:T(1,128)} %bitcast.5, s32[8]{0:T(128)} %lengths_hbm.1, bf16[256,4096]{1,0:T(8,128)(2,1)} %store_ref.1), custom_call_target="tpu_custom_call" | custom-call | flops 4294967296 | bytes 8388608 | tf_op jit(solution)/shard_map/pallas_call | solution.py:656
  69.5 1.3 %copy.9 = f32[8,256]{1,0:T(8,128)} copy(f32[8,256]{1,0:T(8,128)} %shard_map.73) | data formatting | bytes 16384

commit v4 on v3

--- a/solution.py
+++ b/solution.py
@@ -166,6 +166,7 @@
     logits,
     inner,
     store,
+    turned,
     in_proj_ref,
     out_proj_ref,
     targets_ref,
@@ -328,51 +329,31 @@
     def arrived(index, side):
         hop(index, side, 0, me).wait_recv()
 
-    def accumulate(index, start, size):
-        rows = pl.ds(pl.multiple_of(start, 16), size)
-        columns = pl.ds(pl.multiple_of(index * block, block), block)
-        features = feat[index, rows, :]
-        logits[rows, :] += jnp.dot(
-            features, weights[columns, :], preferred_element_type=jnp.float32
-        )
-        inner[rows, :] += lax.dot_general(
-            features,
-            in_proj_ref[:, columns],
-            (((1,), (1,)), ((), ())),
-            preferred_element_type=jnp.float32,
-        )
+    strip = 2 * LANES
 
     def multiply(k):
         zz = nth(k)
+        for pair in (2, 3):
+            for side in range(2):
+                arrived(item(zz, side, pair), side)
         pltpu.make_async_copy(head_chunk(zz), head_chunk(zz), head_recv.at[zz]).wait()
 
+        def wide():
+            return jnp.concatenate([feat[place(zz, at // 2, at % 2)] for at in range(4)], axis=1)
+
+        rows = pl.ds(pl.multiple_of(zz * chunk, chunk), chunk)
+
         def body(step, carry):
-            side, pair = step % 2, step // 2
-            near, far = pair % 2, pair // 2
-            flip_x = (1 - side) * near + side * far
-            flip_y = (1 - side) * far + side * near
-            index = place(zz, (y + flip_y) % 2, (x + flip_x) % 2)
-
-            @pl.when(pair >= 2)
-            def _():
-                pltpu.make_async_copy(
-                    piece(index, 0), piece(index, 0), feat_recv.at[side, index]
-                ).wait()
-
-            accumulate(index, side * long_rows, long_rows)
+            columns = pl.ds(pl.multiple_of(step * strip, strip), strip)
+            product = jnp.dot(wide(), weights[rows, columns], preferred_element_type=jnp.float32)
+            logits[:, columns] = product if k == 0 else logits[:, columns] + product
             return carry
 
-        lax.fori_loop(0, 8, body, 0)
-
-    def multiply_short(k):
-        zz = nth(k)
-
-        def body(pair, carry):
-            index = place(zz, (y + pair // 2) % 2, (x + pair % 2) % 2)
-            accumulate(index, 2 * long_rows, 2 * short_rows)
-            return carry
-
-        lax.fori_loop(0, 4, body, 0)
+        lax.fori_loop(0, vocab_cols // strip, body, 0)
+        product = lax.dot_general(
+            wide(), in_proj_ref[:, rows], (((1,), (1,)), ((), ())), preferred_element_type=jnp.float32
+        )
+        inner[...] = product if k == 0 else inner[...] + product
 
     def short_arrivals(k):
         for pair in range(4):
@@ -447,8 +428,6 @@
         return carry
 
     lax.fori_loop(1, count, send_pick, 0)
-    logits[...] = jnp.zeros_like(logits)
-    inner[...] = jnp.zeros_like(inner)
 
     for k in range(line):
         if k == 1:
@@ -466,17 +445,24 @@
             short_arrivals(k - 1)
         if k == 1:
             local_feat.wait()
+        if k == 1:
+            local_store.wait()
+            turned_columns = 4 * LANES
+
+            def turn(step, carry):
+                columns = pl.ds(pl.multiple_of(step * turned_columns, turned_columns), turned_columns)
+                turned[columns, :] = store[:, columns].astype(jnp.float32).T.astype(jnp.bfloat16)
+                return carry
+
+            lax.fori_loop(0, width * width // turned_columns, turn, 0)
         if k > 1:
             multiply(k - 2)
-            multiply_short(k - 2)
     for side in range(2):
         arrived(item(nth(line - 1), side, 1), side)
         onward(line - 1, side).start()
     multiply(line - 2)
-    multiply_short(line - 2)
     short_arrivals(line - 1)
     multiply(line - 1)
-    multiply_short(line - 1)
 
     lanes = lax.broadcasted_iota(jnp.int32, (TILE, LANES), 1)
     per_tile = TILE // own
@@ -609,12 +595,8 @@
         flat[:, pair * LANES : (pair + 1) * LANES] = jnp.concatenate(
             [even[:, width:], odd[:, width:]], axis=1
         )
-    local_store.wait()
-    scores_ref[...] = lax.dot_general(
-        flat[...].astype(jnp.bfloat16),
-        store[...],
-        (((1,), (1,)), ((), ())),
-        preferred_element_type=jnp.float32,
+    scores_ref[...] = jnp.dot(
+        flat[...].astype(jnp.bfloat16), turned[...], preferred_element_type=jnp.float32
     )
 
     for copy in side_copies + mix_copies:
@@ -644,6 +626,8 @@
         and tokens >= 160
         and TILE % own == 0
         and grad_store.shape[1] == width * width
+        and width * width % (4 * LANES) == 0
+        and vocab_cols % (2 * LANES) == 0
     )
     if not fits:
         return per_device(hidden, head_weight, in_proj, out_proj, targets, lengths, grad_store)
@@ -664,6 +648,7 @@
             pltpu.VMEM((tokens, vocab_cols), f32),
             pltpu.VMEM((tokens, width), f32),
             pltpu.VMEM(grad_store.shape, bf16),
+            pltpu.VMEM(grad_store.shape[::-1], bf16),
             pltpu.VMEM(in_proj.shape[::-1], bf16),
             pltpu.VMEM(out_proj.shape[::-1], bf16),
             pltpu.VMEM((1, tokens), jnp.int32),

time: 71 us -> 68.9 us (0.970)
  Pallas kernels: 69.5 us -> 67.4 us
    pallas_call x1, Pallas kernels: 69.5 us -> 67.4 us  [per_device_any(): pl.pallas_call(functools.partial(kernel, line, parts), out_shape=jax.Shap...]
where the time goes in v4:
time: 68.9 us; the launch traced here: 68.7 us
  Pallas kernels  67.4 us (98%)
  local copies, waits for them, and re-layouts  1.3 us (2%)
    pallas_call x1, Pallas kernels, per_device_any(): pl.pallas_call(functools.partial(kernel, line, parts), out_shape=jax.Shap...  67.4 us

profile of v4, /device:TPU:1, one launch (start us, length us, event | category | flops | bytes accessed | tf_op | source)
XLA Modules:
  0.0 68.7 jit_solution(8128993668150302271)
XLA Ops:
  0.0 67.4 %shard_map.73 = f32[8,256]{1,0:T(8,128)} custom-call(bf16[512,256]{1,0:T(8,128)(2,1)} %hidden_ref.1, bf16[2048,1024]{1,0:T(8,128)(2,1)} %head_ref.1, bf16[64,4096]{1,0:T(8,128)(2,1)} %bitcast.3, bf16[64,1024]{1,0:T(8,128)(2,1)} %bitcast.4, s32[1,512]{1,0:T(1,128)} %bitcast.5, s32[8]{0:T(128)} %lengths_hbm.1, bf16[256,4096]{1,0:T(8,128)(2,1)} %store_ref.1), custom_call_target="tpu_custom_call" | custom-call | flops 4294967296 | bytes 8388608 | tf_op jit(solution)/shard_map/pallas_call | solution.py:640
  67.4 1.3 %copy.9 = f32[8,256]{1,0:T(8,128)} copy(f32[8,256]{1,0:T(8,128)} %shard_map.73) | data formatting | bytes 16384

commit v5 on v4

--- a/solution.py
+++ b/solution.py
@@ -137,13 +137,16 @@
     scaled = (cov + identity * damp) * shrink
     reach = 1.0 / (1.0 + 2.0 * damping_ratio / width)
     gain = 2.0 / (2.0 - reach * reach)
-    inverse = gain * (2.0 * identity - scaled)
+    error = identity - scaled
+    inverse = gain * (identity + error)
+    error = (1.0 - gain) * identity + gain * dot_f32(error, error, ((1,), (0,)))
     reach = reach * reach / (2.0 - reach * reach)
     while reach > 1e-8:
         gain = 2.0 / (2.0 - reach * reach)
         reach = reach * reach / (2.0 - reach * reach)
-        if reach > 1e-3:
-            inverse = gain * (2.0 * inverse - dot_three(inverse, dot_three(scaled, inverse)))
+        if reach > 1e-8:
+            inverse = gain * (inverse + dot_f32(inverse, error, ((1,), (0,))))
+            error = (1.0 - gain) * identity + gain * dot_f32(error, error, ((1,), (0,)))
         else:
             again = dot_f32(scaled, inverse, ((1,), (0,)))
             inverse = gain * (2.0 * inverse - dot_f32(inverse, again, ((1,), (0,))))
@@ -399,70 +402,71 @@
 
     head_sends(lambda copy: copy.start())
 
-    for copy in small:
-        copy.wait()
-    marker = lax.broadcasted_iota(jnp.int32, (LANES - width, vocab_cols), 0)
-    upright = jnp.concatenate([out_proj_ref[...].astype(jnp.float32), (marker == 0).astype(jnp.float32)], axis=0)
-    table[...] = upright.T.astype(jnp.bfloat16)
-    column_ids = lax.broadcasted_iota(jnp.int32, (vocab_cols, tokens), 0) + me * vocab_cols
-    onehot = (column_ids == targets_ref[...]).astype(jnp.float32).astype(jnp.bfloat16)
-    pick[...] = jnp.dot(
-        upright.astype(jnp.bfloat16), onehot, preferred_element_type=jnp.float32
-    ).T.astype(jnp.bfloat16)
-
     def own_part(ref, device):
         return ref.at[pl.ds(pl.multiple_of(device * own, own), own)]
 
     def slot(device):
         return (me - device - 1 + 2 * count) % count
 
-    def send_pick(step, carry):
-        device = (me + step) % count
-        send(
-            own_part(pick, device),
-            pick_in.at[slot(device)],
-            pick_sems.at[0],
-            pick_sems.at[1],
-            {"vocab": device},
-        ).start()
-        return carry
-
-    lax.fori_loop(1, count, send_pick, 0)
-
-    for k in range(line):
-        if k == 1:
-            for pair in (1, 2, 3):
-                for side in (2, 3):
-                    arrived(item(z, side, pair), side)
-                    short_onward(pair, side, lambda copy: copy.start())
-        if k > 0:
-            for side in range(2):
-                arrived(place(nth(k), y, x), side)
-                outward(k, side, lambda copy: copy.start())
-            for side in range(2):
-                arrived(item(nth(k - 1), side, 1), side)
-                onward(k - 1, side).start()
+    def send_targets():
+        for copy in small:
+            copy.wait()
+        marker = lax.broadcasted_iota(jnp.int32, (LANES - width, vocab_cols), 0)
+        upright = jnp.concatenate([out_proj_ref[...].astype(jnp.float32), (marker == 0).astype(jnp.float32)], axis=0)
+        table[...] = upright.T.astype(jnp.bfloat16)
+        column_ids = lax.broadcasted_iota(jnp.int32, (vocab_cols, tokens), 0) + me * vocab_cols
+        onehot = (column_ids == targets_ref[...]).astype(jnp.float32).astype(jnp.bfloat16)
+        pick[...] = jnp.dot(
+            upright.astype(jnp.bfloat16), onehot, preferred_element_type=jnp.float32
+        ).T.astype(jnp.bfloat16)
+
+        def send_pick(step, carry):
+            device = (me + step) % count
+            send(
+                own_part(pick, device),
+                pick_in.at[slot(device)],
+                pick_sems.at[0],
+                pick_sems.at[1],
+                {"vocab": device},
+            ).start()
+            return carry
+
+        lax.fori_loop(1, count, send_pick, 0)
+
+    def turn_store():
+        local_store.wait()
+        turned_columns = 4 * LANES
+
+        def turn(step, carry):
+            columns = pl.ds(pl.multiple_of(step * turned_columns, turned_columns), turned_columns)
+            turned[columns, :] = store[:, columns].astype(jnp.float32).T.astype(jnp.bfloat16)
+            return carry
+
+        lax.fori_loop(0, width * width // turned_columns, turn, 0)
+
+    for pair in (1, 2, 3):
+        for side in (2, 3):
+            arrived(item(z, side, pair), side)
+            short_onward(pair, side, lambda copy: copy.start())
+    for k in range(1, line):
+        for side in range(2):
+            arrived(place(nth(k), y, x), side)
+            outward(k, side, lambda copy: copy.start())
+        for side in range(2):
+            arrived(item(nth(k - 1), side, 1), side)
+            onward(k - 1, side).start()
+        if k > 1:
             short_arrivals(k - 1)
         if k == 1:
-            local_feat.wait()
-        if k == 1:
-            local_store.wait()
-            turned_columns = 4 * LANES
-
-            def turn(step, carry):
-                columns = pl.ds(pl.multiple_of(step * turned_columns, turned_columns), turned_columns)
-                turned[columns, :] = store[:, columns].astype(jnp.float32).T.astype(jnp.bfloat16)
-                return carry
-
-            lax.fori_loop(0, width * width // turned_columns, turn, 0)
-        if k > 1:
-            multiply(k - 2)
+            send_targets()
     for side in range(2):
         arrived(item(nth(line - 1), side, 1), side)
         onward(line - 1, side).start()
-    multiply(line - 2)
     short_arrivals(line - 1)
-    multiply(line - 1)
+    local_feat.wait()
+    turn_store()
+    for k in range(line):
+        multiply(k)
 
     lanes = lax.broadcasted_iota(jnp.int32, (TILE, LANES), 1)
     per_tile = TILE // own

time: 68.9 us -> 72.5 us (1.052)
  Pallas kernels: 67.4 us -> 71 us
    pallas_call x1, Pallas kernels: 67.4 us -> 71 us  [per_device_any(): pl.pallas_call(functools.partial(kernel, line, parts), out_shape=jax.Shap...]
where the time goes in v5:
time: 72.5 us; the launch traced here: 72.3 us
  Pallas kernels  71 us (98%)
  local copies, waits for them, and re-layouts  1.3 us (2%)
    pallas_call x1, Pallas kernels, per_device_any(): pl.pallas_call(functools.partial(kernel, line, parts), out_shape=jax.Shap...  71 us

profile of v5, /device:TPU:1, one launch (start us, length us, event | category | flops | bytes accessed | tf_op | source)
XLA Modules:
  0.0 72.3 jit_solution(5103069954612776060)
XLA Ops:
  0.0 71.0 %shard_map.73 = f32[8,256]{1,0:T(8,128)} custom-call(bf16[512,256]{1,0:T(8,128)(2,1)} %hidden_ref.1, bf16[2048,1024]{1,0:T(8,128)(2,1)} %head_ref.1, bf16[64,4096]{1,0:T(8,128)(2,1)} %bitcast.3, bf16[64,1024]{1,0:T(8,128)(2,1)} %bitcast.4, s32[1,512]{1,0:T(1,128)} %bitcast.5, s32[8]{0:T(128)} %lengths_hbm.1, bf16[256,4096]{1,0:T(8,128)(2,1)} %store_ref.1), custom_call_target="tpu_custom_call" | custom-call | flops 4294967296 | bytes 8388608 | tf_op jit(solution)/shard_map/pallas_call | solution.py:644
  71.0 1.3 %copy.9 = f32[8,256]{1,0:T(8,128)} copy(f32[8,256]{1,0:T(8,128)} %shard_map.73) | data formatting | bytes 16384

commit v6 on v5

--- a/solution.py
+++ b/solution.py
@@ -459,14 +459,17 @@
             short_arrivals(k - 1)
         if k == 1:
             send_targets()
+            local_feat.wait()
+        if k == line - 1:
+            turn_store()
+        if k > 1:
+            multiply(k - 2)
     for side in range(2):
         arrived(item(nth(line - 1), side, 1), side)
         onward(line - 1, side).start()
     short_arrivals(line - 1)
-    local_feat.wait()
-    turn_store()
-    for k in range(line):
-        multiply(k)
+    multiply(line - 2)
+    multiply(line - 1)
 
     lanes = lax.broadcasted_iota(jnp.int32, (TILE, LANES), 1)
     per_tile = TILE // own
@@ -623,6 +626,7 @@
     tiles = tokens // TILE
     fits = (
         count % (4 * parts) == 0
+        and count > 4
         and block % LANES == 0
         and 2 * width == LANES
         and own % 32 == 0

time: 72.5 us -> 67 us (0.924)
  Pallas kernels: 71 us -> 65.5 us
    pallas_call x1, Pallas kernels: 71 us -> 65.5 us  [per_device_any(): pl.pallas_call(functools.partial(kernel, line, parts), out_shape=jax.Shap...]
where the time goes in v6:
time: 67 us; the launch traced here: 66.8 us
  Pallas kernels  65.5 us (98%)
  local copies, waits for them, and re-layouts  1.3 us (2%)
    pallas_call x1, Pallas kernels, per_device_any(): pl.pallas_call(functools.partial(kernel, line, parts), out_shape=jax.Shap...  65.5 us

profile of v6, /device:TPU:1, one launch (start us, length us, event | category | flops | bytes accessed | tf_op | source)
XLA Modules:
  0.0 66.8 jit_solution(12872792854409793697)
XLA Ops:
  0.0 65.5 %shard_map.73 = f32[8,256]{1,0:T(8,128)} custom-call(bf16[512,256]{1,0:T(8,128)(2,1)} %hidden_ref.1, bf16[2048,1024]{1,0:T(8,128)(2,1)} %head_ref.1, bf16[64,4096]{1,0:T(8,128)(2,1)} %bitcast.3, bf16[64,1024]{1,0:T(8,128)(2,1)} %bitcast.4, s32[1,512]{1,0:T(1,128)} %bitcast.5, s32[8]{0:T(128)} %lengths_hbm.1, bf16[256,4096]{1,0:T(8,128)(2,1)} %store_ref.1), custom_call_target="tpu_custom_call" | custom-call | flops 4294967296 | bytes 8388608 | tf_op jit(solution)/shard_map/pallas_call | solution.py:648
  65.5 1.3 %copy.9 = f32[8,256]{1,0:T(8,128)} copy(f32[8,256]{1,0:T(8,128)} %shard_map.73) | data formatting | bytes 16384

commit v7 on v6

--- a/solution.py
+++ b/solution.py
@@ -139,14 +139,14 @@
     gain = 2.0 / (2.0 - reach * reach)
     error = identity - scaled
     inverse = gain * (identity + error)
-    error = (1.0 - gain) * identity + gain * dot_f32(error, error, ((1,), (0,)))
+    error = (1.0 - gain) * identity + gain * dot_three(error, error)
     reach = reach * reach / (2.0 - reach * reach)
     while reach > 1e-8:
         gain = 2.0 / (2.0 - reach * reach)
         reach = reach * reach / (2.0 - reach * reach)
         if reach > 1e-8:
-            inverse = gain * (inverse + dot_f32(inverse, error, ((1,), (0,))))
-            error = (1.0 - gain) * identity + gain * dot_f32(error, error, ((1,), (0,)))
+            inverse = gain * (inverse + dot_three(inverse, error))
+            error = (1.0 - gain) * identity + gain * dot_three(error, error)
         else:
             again = dot_f32(scaled, inverse, ((1,), (0,)))
             inverse = gain * (2.0 * inverse - dot_f32(inverse, again, ((1,), (0,))))
@@ -332,7 +332,7 @@
     def arrived(index, side):
         hop(index, side, 0, me).wait_recv()
 
-    strip = 2 * LANES
+    strip = 4 * LANES
 
     def multiply(k):
         zz = nth(k)
@@ -635,7 +635,7 @@
         and TILE % own == 0
         and grad_store.shape[1] == width * width
         and width * width % (4 * LANES) == 0
-        and vocab_cols % (2 * LANES) == 0
+        and vocab_cols % (4 * LANES) == 0
     )
     if not fits:
         return per_device(hidden, head_weight, in_proj, out_proj, targets, lengths, grad_store)

time: 67 us -> 66 us (0.985)
  Pallas kernels: 65.5 us -> 64.5 us
    pallas_call x1, Pallas kernels: 65.5 us -> 64.5 us  [per_device_any(): pl.pallas_call(functools.partial(kernel, line, parts), out_shape=jax.Shap...]
where the time goes in v7:
time: 66 us; the launch traced here: 65.8 us
  Pallas kernels  64.5 us (98%)
  local copies, waits for them, and re-layouts  1.3 us (2%)
    pallas_call x1, Pallas kernels, per_device_any(): pl.pallas_call(functools.partial(kernel, line, parts), out_shape=jax.Shap...  64.5 us

profile of v7, /device:TPU:1, one launch (start us, length us, event | category | flops | bytes accessed | tf_op | source)
XLA Modules:
  0.0 65.8 jit_solution(1973777934566150227)
XLA Ops:
  0.0 64.5 %shard_map.73 = f32[8,256]{1,0:T(8,128)} custom-call(bf16[512,256]{1,0:T(8,128)(2,1)} %hidden_ref.1, bf16[2048,1024]{1,0:T(8,128)(2,1)} %head_ref.1, bf16[64,4096]{1,0:T(8,128)(2,1)} %bitcast.3, bf16[64,1024]{1,0:T(8,128)(2,1)} %bitcast.4, s32[1,512]{1,0:T(1,128)} %bitcast.5, s32[8]{0:T(128)} %lengths_hbm.1, bf16[256,4096]{1,0:T(8,128)(2,1)} %store_ref.1), custom_call_target="tpu_custom_call" | custom-call | flops 4294967296 | bytes 8388608 | tf_op jit(solution)/shard_map/pallas_call | solution.py:648
  64.5 1.3 %copy.9 = f32[8,256]{1,0:T(8,128)} copy(f32[8,256]{1,0:T(8,128)} %shard_map.73) | data formatting | bytes 16384
